TPU v7x, 512 devices: a whole 4x4x16 slice. The times are simulated.
512 devices in a mesh: inner: 8 (over y_lo, x), outer: 64 (over y_hi, z, core).
Axes of the slice: x: 4, y: 4 (y_hi: 2, y_lo: 2; y = y_hi * 2 + y_lo), z: 16, core: 2. Of those that a mesh axis runs over, the one named last changes fastest.
Arguments:
- tokens: bfloat16 [65536, 4096], P(('inner', 'outer')), may hold values from -24 to 24
- grad_out: bfloat16 [65536, 4096], P(('inner', 'outer')), may hold values from -24 to 24
- quant_weights: bfloat16 [3, 32, 128, 512], P(None, 'inner'), may hold values from -0.09375 to 0.09375
- block_scales: float32 [3, 32, 512], P(None, 'inner'), may hold values from 0.5 to 2
Outputs:
- input_grad: bfloat16 [65536, 4096], P(('inner', 'outer'))
- weight_grads: float32 [3, 4096, 512], P(None, ('inner', 'outer'))
All inputs are finite; a program needn't handle non-finite values.
Results may differ from a plain program's by a relative error of at most 0.028.
Values may be sent and summed in bfloat16 or wider, within the bound.
A program may use at most 128 MiB of HBM per device.

v0:
```python
import jax
import jax.numpy as jnp
from jax import lax
from jax.sharding import PartitionSpec as P


def local(tokens, grad_out, quant_weights, block_scales):
    row_count = tokens.shape[0]
    feature_count = tokens.shape[1]
    hidden_count = quant_weights.shape[3]
    inner_count = lax.axis_size("inner")
    outer_count = lax.axis_size("outer")
    all_values, all_scales = (
        lax.all_gather(quant_weights, "inner", axis=1, tiled=True),
        lax.all_gather(block_scales.astype(jnp.bfloat16), "inner", axis=1, tiled=True).astype(
            block_scales.dtype
        ),
    )
    weights = (all_values.astype(jnp.float32) * all_scales[:, :, None, :]).astype(jnp.bfloat16)
    weights = weights.reshape(3, feature_count, hidden_count)
    gate_pre = jnp.dot(tokens, weights[0], preferred_element_type=jnp.float32)
    up_pre = jnp.dot(tokens, weights[1], preferred_element_type=jnp.float32)
    d_hidden = jnp.dot(grad_out, weights[2], preferred_element_type=jnp.float32)
    sigmoid_gate = jax.nn.sigmoid(gate_pre)
    hidden = (gate_pre * sigmoid_gate * up_pre).astype(jnp.bfloat16)
    grad_up = (d_hidden * gate_pre * sigmoid_gate).astype(jnp.bfloat16)
    grad_gate = (d_hidden * up_pre * sigmoid_gate * (1.0 + gate_pre * (1.0 - sigmoid_gate))).astype(
        jnp.bfloat16
    )
    input_grad = jnp.dot(grad_gate, weights[0].T, preferred_element_type=jnp.float32)
    input_grad = (
        input_grad + jnp.dot(grad_up, weights[1].T, preferred_element_type=jnp.float32)
    ).astype(jnp.bfloat16)
    first = jnp.dot(tokens.T, grad_gate, preferred_element_type=jnp.float32).astype(jnp.bfloat16)
    second = jnp.dot(tokens.T, grad_up, preferred_element_type=jnp.float32).astype(jnp.bfloat16)
    third = jnp.dot(grad_out.T, hidden, preferred_element_type=jnp.float32).astype(jnp.bfloat16)
    partials = jnp.stack([first, second, third])
    owner_rows = feature_count // (inner_count * outer_count)
    outgoing = partials.reshape(3, inner_count, outer_count, owner_rows, hidden_count)
    received = lax.all_to_all(outgoing, "outer", split_axis=2, concat_axis=2, tiled=True)
    across_groups = jnp.sum(received.astype(jnp.float32), axis=2)
    owned_rows = lax.psum_scatter(
        across_groups.astype(jnp.bfloat16), "inner", scatter_dimension=1, tiled=True
    ).astype(jnp.float32)
    owned_rows = owned_rows.reshape(3, owner_rows, hidden_count)
    total_tokens = row_count * inner_count * outer_count
    weight_grads = owned_rows * (1.0 / jnp.sqrt(jnp.float32(total_tokens)))
    return (input_grad, weight_grads)


def solution(mesh):
    return jax.shard_map(
        local,
        mesh=mesh,
        in_specs=(
            P(("inner", "outer"), None),
            P(("inner", "outer"), None),
            P(None, "inner", None, None),
            P(None, "inner", None),
        ),
        out_specs=(P(("inner", "outer"), None), P(None, ("inner", "outer"), None)),
        check_vma=False,
    )
```

profile of v0, /device:TPU:1, one launch (start us, length us, event | category | flops | bytes accessed | tf_op | source)
XLA Modules:
  0.0 864.1 jit_solution(2210645582631419242)
XLA Ops:
  7.9 0.7 convert_element_type.48
  8.7 23.1 %all_gather.7 = bf16[3,32,512]{2,0,1:T(4,128)(2,1)S(1)} all-gather(bf16[3,4,512]{2,0,1:T(4,128)(2,1)S(1)} %copy.23), channel_id=1, replica_groups=mesh['inner'=8,'outer'=64] {'inner'}, dimensions={1}, use_global_device_ids=true | all-gather | bytes 110592 | tf_op jit(solution)/shard_map/all_gather | solution.py:15
  31.8 122.8 %all-gather.2.cloned.1.call-done = bf16[3,32,128,512]{3,2,1,0:T(8,128)(2,1)} async-done(((bf16[3,4,128,512]{3,2,1,0:T(8,128)(2,1)}), bf16[3,32,128,512]{3,2,1,0:T(8,128)(2,1)}) %all-gather.2.cloned.1.call-update) | async-done | bytes 12582928 | tf_op jit(solution)/shard_map/all_gather | solution.py:14
  154.6 7.0 multiply_convert_fusion
  161.6 1.5 fusion.6
  163.2 1.3 convolution_bitcast_fusion
  164.4 1.3 convolution_bitcast_fusion.1
  166.3 3.2 fusion.2
  169.6 1.3 multiply_convert_fusion.2
  170.9 6.5 copy.27
  177.3 3.2 fusion.1
  180.6 6.5 copy.26
  187.1 3.2 fusion
  190.2 6.5 copy.25
  196.7 6.3 pad_maximum_fusion
  203.0 5.4 copy.28
  208.4 15.6 %all-to-all-start = ((bf16[3,8,64,8,512]{4,3,1,0,2:T(8,128)(2,1)}), bf16[3,8,64,8,512]{4,3,1,0,2:T(8,128)(2,1)}, u32[]{:S(2)}, u32[]{:S(2)}) async-start(bf16[3,8,64,8,512]{4,3,1,0,2:T(8,128)(2,1)} %copy.28), calls=%async_computation | async-start | bytes 25165824 | tf_op jit(solution)/shard_map/all_to_all | solution.py:40
  224.2 1.2 dynamic-slice
  225.5 3.7 fusion.7
  229.2 539.6 %all-to-all-done = bf16[3,8,64,8,512]{4,3,1,0,2:T(8,128)(2,1)} async-done(((bf16[3,8,64,8,512]{4,3,1,0,2:T(8,128)(2,1)}), bf16[3,8,64,8,512]{4,3,1,0,2:T(8,128)(2,1)}, u32[]{:S(2)}, u32[]{:S(2)}) %all-to-all-start) | async-done | bytes 12582944 | tf_op jit(solution)/shard_map/all_to_all | solution.py:40
  768.8 7.8 reduce_sum.12
  776.6 4.7 fusion.3
  781.3 74.0 %all-reduce.3.cloned.1.call-done = bf16[3,8,8,512]{3,2,1,0:T(8,128)(2,1)} async-done(((bf16[3,8,8,512]{3,2,1,0:T(8,128)(2,1)}), bf16[3,8,8,512]{3,2,1,0:T(8,128)(2,1)}) %all-reduce.3.cloned.1.call-update) | async-done | bytes 196624
  855.3 1.9 multiply_bitcast_fusion
  (16 shorter events, 1.6 us)
Async XLA Ops:
  7.2 156.0 %copy-start = (bf16[128,4096]{1,0:T(8,128)(2,1)S(1)}, bf16[128,4096]{1,0:T(8,128)(2,1)}, u32[]{:S(2)}) copy-start(bf16[128,4096]{1,0:T(8,128)(2,1)} %param.4) | copy-start | bytes 3145732
  7.2 147.4 %all-gather.2.cloned.1.call-start = ((), (), s32[]{:S(2)}) async-start(), calls=%async_computation.1 | async-start | bytes 14155776 | tf_op jit(solution)/shard_map/all_gather | solution.py:14
  163.1 2.6 copy-start.2
  163.1 3.2 copy-start.3
  163.1 3.2 copy-start.4
  208.4 560.4 %all-to-all-start = ((bf16[3,8,64,8,512]{4,3,1,0,2:T(8,128)(2,1)}), bf16[3,8,64,8,512]{4,3,1,0,2:T(8,128)(2,1)}, u32[]{:S(2)}, u32[]{:S(2)}) async-start(bf16[3,8,64,8,512]{4,3,1,0,2:T(8,128)(2,1)} %copy.28), calls=%async_computation | async-start | bytes 25165824 | tf_op jit(solution)/shard_map/all_to_all | solution.py:40
  224.0 631.3 %all-reduce.3.cloned.1.call-start = ((), (), s32[]{:S(2)}) async-start(), calls=%async_computation.2 | async-start | bytes 393216
  768.8 88.4 %copy-start.1 = (bf16[128,4096]{1,0:T(8,128)(2,1)S(1)}, bf16[128,4096]{1,0:T(8,128)(2,1)}, u32[]{:S(2)}) copy-start(bf16[128,4096]{1,0:T(8,128)(2,1)} %param.4) | copy-start | bytes 3145732
Sparse Core Ops, SparseCore 0:
  10.1 144.4 all-gather.1
  776.8 78.5 all-reduce.2
where the time goes:
time: 869 us; the launch traced here: 864 us
  waiting for transfers between devices  737 us (85%)
  local copies, waits for them, and re-layouts  28.1 us (3%)
  other arithmetic  23.8 us (3%)
  blocking collectives  23.1 us (3%)
  matrix products  21.8 us (3%)
  starting transfers between devices  15.9 us (2%)
  between operations  14.2 us (2%)
    all_to_all x1, waiting for transfers between devices, local(): lax.all_to_all(outgoing, 'outer', split_axis=2, concat_axis=2, tiled=True)  540 us
    all_gather x1, waiting for transfers between devices, local(): lax.all_gather(quant_weights, 'inner', axis=1, tiled=True)  123 us
    unnamed x3, waiting for transfers between devices  74.7 us
    all_gather x1, blocking collectives, local(): lax.all_gather(block_scales.astype(jnp.bfloat16), 'inner', axis=1, tiled=...  23.1 us
  transfers between devices with their start and end apart: 3, of which 3 were waited for; matrix products, arithmetic and copies ran while one was open for 1% of the time, Pallas kernels for 0%

commit v1 on v0

v1 whole, which is shorter than its diff:
```python
import functools

import jax
import jax.numpy as jnp
from jax import lax
from jax.experimental import pallas as pl
from jax.experimental.pallas import tpu as pltpu
from jax.sharding import PartitionSpec as P

MESH = pl.DeviceIdType.MESH
BF16, F32 = jnp.bfloat16, jnp.float32
NX, NY, NZ = 4, 4, 16
TOK = 128
HALF = 2048
HK = 256
Q = 256
NT = (((1,), (1,)), ((), ()))


def aligned(index, size):
    return pl.ds(pl.multiple_of(index * size, size), size)


def dot(a, b):
    return jnp.dot(a, b, preferred_element_type=F32)


def kernel(
    tok_hbm, out_hbm, quant_hbm, scales,
    ig_hbm, wg_ref,
    xt, xg, quant, w, pacc, psend, precv, gn, gt, dws, own, relay, near, far,
    ysend, yrecv, zsend, zrecv, fsend, frecv, igk, igs, igr, igo,
    local_sem, xs_sem, xr_sem, ws_sem, wr_sem, ps_sem, pr_sem, rs_sem, rr_sem,
    ys_sem, yr_sem, zs_sem, zr_sem, is_sem, ir_sem, fs_sem, fr_sem,
):
    inner, outer = lax.axis_index("inner"), lax.axis_index("outer")
    x, y_lo = lax.rem(inner, NX), lax.div(inner, NX)
    core, z = lax.rem(outer, 2), lax.rem(lax.div(outer, 2), NZ)
    y_hi = lax.div(outer, 2 * NZ)
    y = 2 * y_hi + y_lo
    other = 1 - core

    def device(dx=0, dy=0, dz=0, at=core):
        to_x, to_y, to_z = (
            lax.rem(x + dx + NX, NX),
            lax.rem(y + dy + NY, NY),
            lax.rem(z + dz + NZ, NZ),
        )
        return (
            lax.rem(to_y, 2) * NX + to_x,
            (lax.div(to_y, 2) * NZ + to_z) * 2 + at,
        )

    sent = []

    def send(src, dst, s_sem, r_sem, to):
        copy = pltpu.make_async_remote_copy(
            src_ref=src, dst_ref=dst, send_sem=s_sem, recv_sem=r_sem, device_id=to, device_id_type=MESH
        )
        copy.start()
        sent.append((src, s_sem))

    def wait(ref, sem):
        pltpu.make_async_copy(ref, ref, sem).wait()

    side = 1 - 2 * core
    mine, theirs = aligned(y_lo, HALF), aligned(1 - y_lo, HALF)
    hidden_half = aligned(core, HK)

    own_rows = aligned(3 * core, TOK)
    pltpu.make_async_copy(quant_hbm.at[:, :, :, hidden_half], quant, local_sem.at[0]).start()
    pltpu.make_async_copy(tok_hbm.at[:, mine], xt.at[own_rows, :], local_sem.at[1]).start()
    pltpu.make_async_copy(out_hbm.at[:, mine], xg.at[own_rows, :], local_sem.at[2]).start()

    barrier = pltpu.get_barrier_semaphore()
    partners = [
        device(at=other), device(dx=1), device(dx=-1), device(dy=1), device(dy=-1), device(dy=2),
        device(dy=side, at=other),
    ]
    for to in partners:
        pl.semaphore_signal(barrier, inc=1, device_id=to, device_id_type=MESH)

    def greet(j, carry):
        pl.semaphore_signal(barrier, inc=1, device_id=device(dz=j), device_id_type=MESH)
        return carry

    lax.fori_loop(1, NZ, greet, 0)
    pl.semaphore_wait(barrier, len(partners) + NZ - 1)

    def send_tokens(a, src, dst):
        away = aligned(2 - core, TOK)
        for part in range(2):
            rows = pl.ds(part * 64, 64)
            to_rows = pl.ds(pl.multiple_of((2 - core) * TOK + part * 64, 64), 64)
            send(
                src.at[rows, theirs], dst.at[to_rows, :], xs_sem.at[a, part], xr_sem.at[a, core],
                device(dy=side, at=part),
            )
        send(src.at[:, mine], dst.at[own_rows, :], xs_sem.at[a, 2], xr_sem.at[a, 2], device(at=other))

    def dequantise(m):
        for b in range(4):
            scale = scales[m, pl.ds(b, 1), hidden_half]
            w[m, x, b * 128 : (b + 1) * 128, :] = (quant[m, b].astype(F32) * scale).astype(BF16)

    def send_weights(m):
        block = w.at[m, x]
        send(block, block, ws_sem.at[m, 0], wr_sem.at[m, 0], device(dx=1))
        send(block, block, ws_sem.at[m, 1], wr_sem.at[m, 1], device(dx=-1))

    before, after = lax.rem(x + 3, NX), lax.rem(x + 1, NX)
    across = lax.rem(x + 2, NX)

    def relay_weights(m):
        wait(w.at[m, before], wr_sem.at[m, 0])
        block = w.at[m, before, pl.ds(0, Q), :]
        send(block, block, ws_sem.at[m, 2], wr_sem.at[m, 2], device(dx=1))
        wait(w.at[m, after], wr_sem.at[m, 1])
        block = w.at[m, after, pl.ds(Q, Q), :]
        send(block, block, ws_sem.at[m, 3], wr_sem.at[m, 3], device(dx=-1))

    wait(quant, local_sem.at[0])
    send_tokens(0, tok_hbm, xt)
    dequantise(0)
    send_weights(0)
    dequantise(1)
    send_weights(1)
    dequantise(2)
    send_tokens(1, out_hbm, xg)

    def pass_tokens(a, dst):
        for i, block in enumerate((2, 1)):
            rows = pl.ds(pl.multiple_of(block * TOK + core * 64, 64), 64)
            wait(dst.at[rows, :], xr_sem.at[a, i])
            send(dst.at[rows, :], dst.at[rows, :], xs_sem.at[a, 3 + i], xr_sem.at[a, 3 + i], device(at=other))

    def wait_tokens(a, dst):
        wait(dst.at[own_rows, :], local_sem.at[1 + a])
        wait(dst.at[aligned(3 - 3 * core, TOK), :], xr_sem.at[a, 2])
        for i, block in enumerate((2, 1)):
            rows = pl.ds(pl.multiple_of(block * TOK + other * 64, 64), 64)
            wait(dst.at[rows, :], xr_sem.at[a, 3 + i])

    def term(m, block):
        rows = (xg if m == 2 else xt)[:, aligned(block, 512)]
        return dot(rows, w[m, block])

    def first_terms(m):
        pacc[m] = term(m, x) + term(m, before) + term(m, after)

    def last_term(m):
        wait(w.at[m, across, pl.ds(0, Q), :], wr_sem.at[m, 2])
        wait(w.at[m, across, pl.ds(Q, Q), :], wr_sem.at[m, 3])
        total = pacc[m] + term(m, across)
        pacc[m] = total
        psend[m] = total.astype(BF16)
        send(psend.at[m, pl.ds(0, 256)], precv.at[m, pl.ds(256, 256)], ps_sem.at[m, 0], pr_sem.at[m, 0], device(dy=1))
        send(psend.at[m, pl.ds(256, 256)], precv.at[m, pl.ds(0, 256)], ps_sem.at[m, 1], pr_sem.at[m, 1], device(dy=-1))

    relay_weights(0)
    send_weights(2)
    pass_tokens(0, xt)
    wait_tokens(0, xt)
    first_terms(0)
    relay_weights(1)
    first_terms(1)
    pass_tokens(1, xg)
    last_term(0)
    wait_tokens(1, xg)
    relay_weights(2)
    first_terms(2)
    last_term(1)
    last_term(2)

    for m in range(3):
        wait(precv.at[m, pl.ds(256, 256)], pr_sem.at[m, 0])
        wait(precv.at[m, pl.ds(0, 256)], pr_sem.at[m, 1])

    def elementwise(b, carry):
        rows = aligned(b, 128)
        gate, up, d_hidden = (pacc[m, rows, :] + precv[m, rows, :].astype(F32) for m in range(3))
        s = jax.nn.sigmoid(gate)
        hidden = (gate * s * up).astype(BF16)
        grad_up = (d_hidden * gate * s).astype(BF16)
        grad_gate = (d_hidden * up * s * (1.0 + gate * (1.0 - s))).astype(BF16)
        gn[0, rows, :] = grad_gate
        gn[1, rows, :] = grad_up
        gt[0, :, rows] = grad_gate.T
        gt[1, :, rows] = grad_up.T
        gt[2, :, rows] = hidden.T
        return carry

    lax.fori_loop(0, 4, elementwise, 0)

    def product(m, block, half):
        columns = aligned(block * 2 + half, Q)
        return dot(gt[m], (xg if m == 2 else xt)[:, columns])

    def send_across(m):
        for half, step in ((0, 1), (1, -1)):
            dws[m, half] = product(m, across, half).astype(BF16)
            send(dws.at[m, half], relay.at[m, half], rs_sem.at[m, half], rr_sem.at[m, half], device(dx=step))

    def send_near(m):
        for half, step, block in ((0, -1, before), (1, 1, after)):
            dws[m, 2 + half] = product(m, block, half).astype(BF16)
            send(
                dws.at[m, 2 + half], near.at[m, half], rs_sem.at[m, 2 + half], rr_sem.at[m, 2 + half],
                device(dx=step),
            )

    def send_far(m):
        for half, step, block in ((0, 1, after), (1, -1, before)):
            value = product(m, block, half)
            wait(relay.at[m, half], rr_sem.at[m, half])
            dws[m, 4 + half] = (value + relay[m, half].astype(F32)).astype(BF16)
            send(
                dws.at[m, 4 + half], far.at[m, half], rs_sem.at[m, 4 + half], rr_sem.at[m, 4 + half],
                device(dx=step),
            )

    def keep(m):
        for half in range(2):
            own[m, half] = product(m, x, half)

    def across_y(m):
        for half in range(2):
            wait(near.at[m, half], rr_sem.at[m, 2 + half])
            wait(far.at[m, half], rr_sem.at[m, 4 + half])
        gone = 1 - y_hi
        ysend[m] = (own[m, gone] + near[m, gone].astype(F32) + far[m, gone].astype(F32)).astype(BF16)
        send(ysend.at[m], yrecv.at[m], ys_sem.at[m], yr_sem.at[m], device(dy=2))
        own[m, y_hi] = own[m, y_hi] + near[m, y_hi].astype(F32) + far[m, y_hi].astype(F32)

    def across_z(m):
        wait(yrecv.at[m], yr_sem.at[m])
        total = own[m, y_hi] + yrecv[m].astype(F32)
        zsend[m] = total.T.astype(BF16).reshape(NZ, 16, HK)

        def post(j, carry):
            to_z = lax.rem(z + j, NZ)
            pltpu.make_async_remote_copy(
                src_ref=zsend.at[m, to_z], dst_ref=zrecv.at[m, j - 1], send_sem=zs_sem.at[m],
                recv_sem=zr_sem.at[m], device_id=device(dz=j), device_id_type=MESH,
            ).start()
            return carry

        lax.fori_loop(1, NZ, post, 0)

    def input_grad(b, carry):
        columns = aligned(b, Q)
        block, half = lax.div(b, 2), lax.rem(b, 2)
        rows = aligned(half, Q)
        total = lax.dot_general(gn[0], w[0, block, rows, :], NT, preferred_element_type=F32)
        total += lax.dot_general(gn[1], w[1, block, rows, :], NT, preferred_element_type=F32)

        @pl.when(core == 0)
        def _():
            igk[0, :, columns] = total[0:128]
            igk[1, :, columns] = total[256:384]
            igs[0, :, columns] = total[384:512].astype(BF16)
            igs[1, :, columns] = total[128:256].astype(BF16)

        @pl.when(core == 1)
        def _():
            igk[0, :, columns] = total[384:512]
            igk[1, :, columns] = total[128:256]
            igs[0, :, columns] = total[0:128].astype(BF16)
            igs[1, :, columns] = total[256:384].astype(BF16)

        return carry

    send_across(0)
    send_near(0)
    send_across(1)
    send_far(0)
    send_near(1)
    send_across(2)
    keep(0)
    send_far(1)
    send_near(2)
    keep(1)
    send_far(2)
    keep(2)
    lax.fori_loop(0, 8, input_grad, 0)
    send(igs, igr, is_sem.at[0], ir_sem.at[0], device(at=other))
    across_y(0)
    wait(igr, ir_sem.at[0])
    for slot in range(2):
        igo[slot] = (igk[slot] + igr[slot].astype(F32)).astype(BF16)
    done = pltpu.make_async_copy(igo.at[0], ig_hbm.at[:, mine], local_sem.at[3])
    done.start()
    send(igo.at[1], ig_hbm.at[:, mine], is_sem.at[1], ir_sem.at[1], device(dy=-side))
    across_z(0)
    across_y(1)
    across_z(1)
    across_y(2)
    across_z(2)

    scale = 1.0 / 256.0
    finals = []
    for m in range(3):
        wait(zrecv.at[m], zr_sem.at[m])
        total = zsend[m, z].astype(F32)
        for j in range(NZ - 1):
            total = total + zrecv[m, j].astype(F32)
        finals.append(total * scale)

    @pl.when(core == 0)
    def _():
        for m in range(3):
            wg_ref[m, :, 0:HK] = finals[m][0:8]
            fsend[m] = finals[m][8:16]

    @pl.when(core == 1)
    def _():
        for m in range(3):
            wg_ref[m, :, HK : 2 * HK] = finals[m][8:16]
            fsend[m] = finals[m][0:8]

    send(fsend, frecv, fs_sem, fr_sem, device(at=other))
    wait(frecv, fr_sem)

    @pl.when(core == 0)
    def _():
        wg_ref[:, :, HK : 2 * HK] = frecv[...]

    @pl.when(core == 1)
    def _():
        wg_ref[:, :, 0:HK] = frecv[...]

    done.wait()
    wait(ig_hbm.at[:, theirs], ir_sem.at[1])
    for m in range(3):
        wait(zrecv.at[m], zs_sem.at[m])
    for src, sem in sent:
        wait(src, sem)


def local(tokens, grad_out, quant_weights, block_scales):
    any_space = pl.BlockSpec(memory_space=pl.ANY)
    vmem = pl.BlockSpec(memory_space=pltpu.VMEM)
    dma = pltpu.SemaphoreType.DMA
    return pl.pallas_call(
        kernel,
        out_shape=(
            jax.ShapeDtypeStruct((TOK, 2 * HALF), BF16),
            jax.ShapeDtypeStruct((3, 8, 2 * HK), F32),
        ),
        in_specs=[any_space, any_space, any_space, vmem],
        out_specs=(any_space, vmem),
        scratch_shapes=[
            pltpu.VMEM((4 * TOK, HALF), BF16),
            pltpu.VMEM((4 * TOK, HALF), BF16),
            pltpu.VMEM((3, 4, 128, HK), BF16),
            pltpu.VMEM((3, NX, 512, HK), BF16),
            pltpu.VMEM((3, 4 * TOK, HK), F32),
            pltpu.VMEM((3, 4 * TOK, HK), BF16),
            pltpu.VMEM((3, 4 * TOK, HK), BF16),
            pltpu.VMEM((2, 4 * TOK, HK), BF16),
            pltpu.VMEM((3, HK, 4 * TOK), BF16),
            pltpu.VMEM((3, 6, HK, Q), BF16),
            pltpu.VMEM((3, 2, HK, Q), F32),
            pltpu.VMEM((3, 2, HK, Q), BF16),
            pltpu.VMEM((3, 2, HK, Q), BF16),
            pltpu.VMEM((3, 2, HK, Q), BF16),
            pltpu.VMEM((3, HK, Q), BF16),
            pltpu.VMEM((3, HK, Q), BF16),
            pltpu.VMEM((3, NZ, 16, HK), BF16),
            pltpu.VMEM((3, NZ - 1, 16, HK), BF16),
            pltpu.VMEM((3, 8, HK), F32),
            pltpu.VMEM((3, 8, HK), F32),
            pltpu.VMEM((2, TOK, HALF), F32),
            pltpu.VMEM((2, TOK, HALF), BF16),
            pltpu.VMEM((2, TOK, HALF), BF16),
            pltpu.VMEM((2, TOK, HALF), BF16),
            dma((4,)),
            dma((2, 5)), dma((2, 5)),
            dma((3, 4)), dma((3, 4)),
            dma((3, 2)), dma((3, 2)),
            dma((3, 6)), dma((3, 6)),
            dma((3,)), dma((3,)),
            dma((3,)), dma((3,)),
            dma((2,)), dma((2,)),
            dma, dma,
        ],
        compiler_params=pltpu.CompilerParams(
            collective_id=0, has_side_effects=True, vmem_limit_bytes=56 * 1024 * 1024
        ),
    )(tokens, grad_out, quant_weights, block_scales)


def solution(mesh):
    return jax.shard_map(
        local,
        mesh=mesh,
        in_specs=(
            P(("inner", "outer"), None),
            P(("inner", "outer"), None),
            P(None, "inner", None, None),
            P(None, "inner", None),
        ),
        out_specs=(P(("inner", "outer"), None), P(None, ("inner", "outer"), None)),
        check_vma=False,
    )
```

time: 869 us -> 110 us (0.13)
  waiting for transfers between devices: 737 us -> 0 us
  Pallas kernels: 0 us -> 106 us
  local copies, waits for them, and re-layouts: 28.1 us -> 2.92 us
  other arithmetic: 23.8 us -> 0 us
  blocking collectives: 23.1 us -> 0 us
  matrix products: 21.8 us -> 0 us
  starting transfers between devices: 15.9 us -> 0 us
  between operations: 14.2 us -> 0.65 us
    all_to_all x1 -> x0, waiting for transfers between devices: 540 us -> none  [local(): lax.all_to_all(outgoing, 'outer', split_axis=2, concat_axis=2, tiled=True)]
    all_gather x1 -> x0, waiting for transfers between devices: 123 us -> none  [local(): lax.all_gather(quant_weights, 'inner', axis=1, tiled=True)]
    pallas_call x0 -> x1, Pallas kernels: none -> 106 us  [local(): pl.pallas_call(kernel, out_shape=(jax.ShapeDtypeStruct((TOK, 2 * HALF), B...]
    unnamed x3 -> x0, waiting for transfers between devices: 74.7 us -> none
    all_gather x1 -> x0, blocking collectives: 23.1 us -> none  [local(): lax.all_gather(block_scales.astype(jnp.bfloat16), 'inner', axis=1, tiled=...]
    dot_general x8 -> x0, matrix products: 21.8 us -> none  [the longest x1 4.66 us: local(): jnp.dot(grad_up, weights[1].T, preferred_element_type=jnp.float32)]
    convert_element_type x4 -> x0, local copies, waits for them, and re-layouts: 19.4 us -> none  [the longest x1 6.5 us: local(): jnp.dot(tokens.T, grad_up, preferred_element_type=jnp.float32)]
    all_to_all x1 -> x0, starting transfers between devices: 15.6 us -> none  [local(): lax.all_to_all(outgoing, 'outer', split_axis=2, concat_axis=2, tiled=True)]
  transfers between devices with their start and end apart: 3 -> 0, of which waited for: 3 -> 0; matrix products, arithmetic and copies ran while one was open for 1% -> 0% of each run, Pallas kernels for 0% -> 0%
where the time goes in v1:
time: 110 us; the launch traced here: 109 us
  Pallas kernels  106 us (96%)
  local copies, waits for them, and re-layouts  2.92 us (3%)
    pallas_call x1, Pallas kernels, local(): pl.pallas_call(kernel, out_shape=(jax.ShapeDtypeStruct((TOK, 2 * HALF), B...  106 us
    unnamed x4, local copies, waits for them, and re-layouts  2.92 us

profile of v1, /device:TPU:1, one launch (start us, length us, event | category | flops | bytes accessed | tf_op | source)
XLA Modules:
  0.0 109.5 jit_solution(15709384371097541410)
XLA Ops:
  0.6 105.9 %shard_map.59 = (bf16[128,4096]{1,0:T(8,128)(2,1)}, f32[3,8,512]{2,1,0:T(8,128)}) custom-call(bf16[128,4096]{1,0:T(8,128)(2,1)} %tok_hbm.1, bf16[128,4096]{1,0:T(8,128)(2,1)} %out_hbm.1, bf16[3,4,128,512]{3,2,1,0:T(8,128)(2,1)} %quant_hbm.1, f32[3,4,512]{2,1,0:T(4,128)} %scales.1), custom_call_target="tpu_custom_call" | custom-call | tf_op jit(solution)/shard_map/pallas_call | solution.py:344
  106.6 0.0 copy-start
  106.6 2.3 %copy.8 = bf16[128,4096]{1,0:T(8,128)(2,1)} copy(bf16[128,4096]{1,0:T(8,128)(2,1)} %get-tuple-element.4) | data formatting | bytes 2097152
  108.9 0.0 copy-done
  108.9 0.6 copy.9
Async XLA Ops:
  106.6 2.3 %copy-start = (f32[3,8,512]{2,1,0:T(8,128)S(1)}, f32[3,8,512]{2,1,0:T(8,128)}, u32[]{:S(2)}) copy-start(f32[3,8,512]{2,1,0:T(8,128)} %get-tuple-element.5) | copy-start | bytes 147460

commit v2 on v1

v2 whole, which is shorter than its diff:
```python
import jax
import jax.numpy as jnp
from jax import lax
from jax.experimental import pallas as pl
from jax.experimental.pallas import tpu as pltpu
from jax.sharding import PartitionSpec as P

MESH = pl.DeviceIdType.MESH
BF16, F32 = jnp.bfloat16, jnp.float32
NX, NY, NZ = 4, 4, 16
TOK = 128
HALF = 2048
HK = 256
Q = 256
WIDTH = (256, 128, 128)
NT = (((1,), (1,)), ((), ()))


def scratch():
    vmem, dma = pltpu.VMEM, pltpu.SemaphoreType.DMA
    shapes = {
        "xt": vmem((4 * TOK, HALF), BF16),
        "xg": vmem((4 * TOK, HALF), BF16),
        "quant": vmem((3, 4, 128, HK), BF16),
        "w": vmem((3, NX, 512, HK), BF16),
        "pacc": vmem((3, 4 * TOK, HK), F32),
        "psend": vmem((3, 4 * TOK, HK), BF16),
        "precv": vmem((3, 4 * TOK, HK), BF16),
        "gn": vmem((2, 4 * TOK, HK), BF16),
        "gt": vmem((3, HK, 4 * TOK), BF16),
        "pair_keep": vmem((3, NX, 2, HK, 128), F32),
        "pair_send": vmem((3, NX, 2, HK, 128), BF16),
        "pair_recv": vmem((3, NX, 2, HK, 128), BF16),
        "fsend": vmem((3, 8, HK), F32),
        "frecv": vmem((3, 8, HK), F32),
        "igk": vmem((2, TOK, HALF), F32),
        "igs": vmem((2, TOK, HALF), BF16),
        "igr": vmem((2, TOK, HALF), BF16),
        "igo": vmem((2, TOK, HALF), BF16),
        "local_sem": dma((4,)),
        "xs_sem": dma((2, 5)), "xr_sem": dma((2, 5)),
        "ws_sem": dma((3, 10)), "wr_sem": dma((3, 10)),
        "ps_sem": dma((3, 2)), "pr_sem": dma((3, 2)),
        "cs_sem": dma((3, NX, 2)), "cr_sem": dma((3, NX, 2)),
        "rs_sem": dma((3, 6)), "rr_sem": dma((3, 6)),
        "ys_sem": dma((3,)), "yr_sem": dma((3,)),
        "zs_sem": dma((3, NZ)), "zr_sem": dma((3, NZ)),
        "is_sem": dma((2,)), "ir_sem": dma((2,)),
        "fs_sem": dma, "fr_sem": dma,
    }
    for m, width in enumerate(WIDTH):
        shapes |= {
            f"dws{m}": vmem((6, HK, width), BF16),
            f"own{m}": vmem((2, HK, width), F32),
            f"relay{m}": vmem((2, HK, width), BF16),
            f"near{m}": vmem((2, HK, width), BF16),
            f"far{m}": vmem((2, HK, width), BF16),
            f"ysend{m}": vmem((HK, width), BF16),
            f"yrecv{m}": vmem((HK, width), BF16),
            f"zsend{m}": vmem((width // 16, 16, HK), BF16),
            f"zrecv{m}": vmem((width // 16, 16, HK), BF16),
        }
    return shapes


def aligned(index, size):
    return pl.ds(pl.multiple_of(index * size, size), size)


def dot(a, b):
    return jnp.dot(a, b, preferred_element_type=F32)


def kernel(tok_hbm, out_hbm, quant_hbm, scales, ig_hbm, wg_ref, *scratch_refs):
    r = dict(zip(scratch(), scratch_refs, strict=True))
    xt, xg, quant, w, pacc, psend, precv, gn, gt = (
        r[name] for name in ("xt", "xg", "quant", "w", "pacc", "psend", "precv", "gn", "gt")
    )
    pair_keep, pair_send, pair_recv = r["pair_keep"], r["pair_send"], r["pair_recv"]
    fsend, frecv, igk, igs, igr, igo = (r[name] for name in ("fsend", "frecv", "igk", "igs", "igr", "igo"))
    local_sem, xs_sem, xr_sem, ws_sem, wr_sem = (
        r[name] for name in ("local_sem", "xs_sem", "xr_sem", "ws_sem", "wr_sem")
    )
    dws, own, relay, near, far, ysend, yrecv, zsend, zrecv = (
        [r[f"{name}{m}"] for m in range(3)]
        for name in ("dws", "own", "relay", "near", "far", "ysend", "yrecv", "zsend", "zrecv")
    )

    inner, outer = lax.axis_index("inner"), lax.axis_index("outer")
    x, y_lo = lax.rem(inner, NX), lax.div(inner, NX)
    core, z = lax.rem(outer, 2), lax.rem(lax.div(outer, 2), NZ)
    y_hi = lax.div(outer, 2 * NZ)
    y = 2 * y_hi + y_lo
    other = 1 - core
    odd = lax.rem(z, 2)
    before, after, across = (lax.rem(x + step, NX) for step in (3, 1, 2))

    def device(dx=0, dy=0, dz=0, at=core):
        to_x, to_y, to_z = (
            lax.rem(x + dx + NX, NX),
            lax.rem(y + dy + NY, NY),
            lax.rem(z + dz + NZ, NZ),
        )
        return (
            lax.rem(to_y, 2) * NX + to_x,
            (lax.div(to_y, 2) * NZ + to_z) * 2 + at,
        )

    sent = []

    def send(src, dst, s_sem, r_sem, to):
        pltpu.make_async_remote_copy(
            src_ref=src, dst_ref=dst, send_sem=s_sem, recv_sem=r_sem, device_id=to, device_id_type=MESH
        ).start()
        sent.append((src, s_sem))

    def wait(ref, sem):
        pltpu.make_async_copy(ref, ref, sem).wait()

    side = 1 - 2 * core
    mine, theirs = aligned(y_lo, HALF), aligned(1 - y_lo, HALF)
    hidden_half = aligned(core, HK)

    own_rows = aligned(3 * core, TOK)
    pltpu.make_async_copy(quant_hbm.at[:, :, :, hidden_half], quant, local_sem.at[0]).start()
    pltpu.make_async_copy(tok_hbm.at[:, mine], xt.at[own_rows, :], local_sem.at[1]).start()
    pltpu.make_async_copy(out_hbm.at[:, mine], xg.at[own_rows, :], local_sem.at[2]).start()

    barrier = pltpu.get_barrier_semaphore()
    partners = [
        device(at=other), device(dx=1), device(dx=-1), device(dy=1), device(dy=-1), device(dy=2),
        device(dy=side, at=other),
    ]
    for to in partners:
        pl.semaphore_signal(barrier, inc=1, device_id=to, device_id_type=MESH)

    def greet(j, carry):
        pl.semaphore_signal(barrier, inc=1, device_id=device(dz=j), device_id_type=MESH)
        return carry

    lax.fori_loop(1, NZ, greet, 0)

    def dequantise(m):
        for b in range(4):
            scale = scales[m, pl.ds(b, 1), hidden_half]
            w[m, x, b * 128 : (b + 1) * 128, :] = (quant[m, b].astype(F32) * scale).astype(BF16)

    wait(quant, local_sem.at[0])
    dequantise(0)
    pl.semaphore_wait(barrier, len(partners) + NZ - 1)

    def send_tokens(a, src, dst):
        for part in range(2):
            rows = pl.ds(part * 64, 64)
            to_rows = pl.ds(pl.multiple_of((2 - core) * TOK + part * 64, 64), 64)
            send(
                src.at[rows, theirs], dst.at[to_rows, :], xs_sem.at[a, part], xr_sem.at[a, core],
                device(dy=side, at=part),
            )
        send(src.at[:, mine], dst.at[own_rows, :], xs_sem.at[a, 2], xr_sem.at[a, 2], device(at=other))

    def pass_tokens(a, dst):
        for i, block in enumerate((2, 1)):
            rows = pl.ds(pl.multiple_of(block * TOK + core * 64, 64), 64)
            wait(dst.at[rows, :], xr_sem.at[a, i])
            send(dst.at[rows, :], dst.at[rows, :], xs_sem.at[a, 3 + i], xr_sem.at[a, 3 + i], device(at=other))

    def wait_tokens(a, dst):
        wait(dst.at[own_rows, :], local_sem.at[1 + a])
        wait(dst.at[aligned(3 - 3 * core, TOK), :], xr_sem.at[a, 2])
        for i, block in enumerate((2, 1)):
            rows = pl.ds(pl.multiple_of(block * TOK + other * 64, 64), 64)
            wait(dst.at[rows, :], xr_sem.at[a, 3 + i])

    def quarter(m, shard, half, q):
        return w.at[m, shard, pl.ds(pl.multiple_of(half * 256 + q * 128, 128), 128), :]

    def half_of(m, shard):
        return w.at[m, shard, aligned(odd, 256), :]

    def pass_on(m, ref, channel, to):
        send(ref, ref, ws_sem.at[m, channel], wr_sem.at[m, channel], to)

    def send_weights(m):
        pass_on(m, half_of(m, x), 0, device(dx=1))
        pass_on(m, half_of(m, x), 1, device(dx=-1))

    def relay_weights(m):
        for i, (shard, step) in enumerate(((before, 1), (after, -1))):
            wait(half_of(m, shard), wr_sem.at[m, i])
            pass_on(m, quarter(m, shard, odd, i), 2 + i, device(dx=step))
            pass_on(m, quarter(m, shard, odd, 0), 4 + 2 * i, device(dz=1))
            pass_on(m, quarter(m, shard, odd, 1), 5 + 2 * i, device(dz=-1))

    def relay_across(m):
        for q, step in ((0, 1), (1, -1)):
            wait(quarter(m, across, odd, q), wr_sem.at[m, 2 + q])
            pass_on(m, quarter(m, across, odd, q), 8 + q, device(dz=step))

    def term(m, shard, half):
        columns = aligned(shard * 2 + half, 256)
        return dot((xg if m == 2 else xt)[:, columns], w[m, shard, aligned(half, 256), :])

    def first_terms(m):
        pacc[m] = term(m, x, 0) + term(m, x, 1) + term(m, before, odd) + term(m, after, odd)

    def last_terms(m):
        for i, shard in enumerate((before, after, across)):
            for q in range(2):
                wait(quarter(m, shard, 1 - odd, q), wr_sem.at[m, 4 + 2 * i + q])
        total = (
            pacc[m] + term(m, before, 1 - odd) + term(m, after, 1 - odd)
            + term(m, across, 0) + term(m, across, 1)
        )
        pacc[m] = total
        psend[m] = total.astype(BF16)
        low, high = pl.ds(0, 256), pl.ds(256, 256)
        send(psend.at[m, low], precv.at[m, high], r["ps_sem"].at[m, 0], r["pr_sem"].at[m, 0], device(dy=1))
        send(psend.at[m, high], precv.at[m, low], r["ps_sem"].at[m, 1], r["pr_sem"].at[m, 1], device(dy=-1))

    send_weights(0)
    send_tokens(0, tok_hbm, xt)
    dequantise(1)
    send_weights(1)
    send_tokens(1, out_hbm, xg)
    dequantise(2)
    relay_weights(0)
    send_weights(2)
    relay_weights(1)
    relay_across(0)
    pass_tokens(0, xt)
    relay_weights(2)
    relay_across(1)
    wait_tokens(0, xt)
    first_terms(0)
    relay_across(2)
    last_terms(0)
    first_terms(1)
    pass_tokens(1, xg)
    last_terms(1)
    wait_tokens(1, xg)
    first_terms(2)
    last_terms(2)

    for m in range(3):
        wait(precv.at[m, pl.ds(256, 256)], r["pr_sem"].at[m, 0])
        wait(precv.at[m, pl.ds(0, 256)], r["pr_sem"].at[m, 1])

    def elementwise(b, carry):
        rows = aligned(b, 128)
        gate, up, d_hidden = (pacc[m, rows, :] + precv[m, rows, :].astype(F32) for m in range(3))
        s = jax.nn.sigmoid(gate)
        hidden = (gate * s * up).astype(BF16)
        grad_up = (d_hidden * gate * s).astype(BF16)
        grad_gate = (d_hidden * up * s * (1.0 + gate * (1.0 - s))).astype(BF16)
        gn[0, rows, :] = grad_gate
        gn[1, rows, :] = grad_up
        gt[0, :, rows] = grad_gate.T
        gt[1, :, rows] = grad_up.T
        gt[2, :, rows] = hidden.T
        return carry

    lax.fori_loop(0, 4, elementwise, 0)

    def product(m, block, half):
        return dot(gt[m], (xg if m == 2 else xt)[:, aligned(block * 2 + half, Q)])

    def pair(m, block):
        for half in range(2):
            value = product(m, block, half)
            low, high = value[:, :128], value[:, 128:]
            pair_keep[m, block, half] = jnp.where(odd == 0, low, high)
            pair_send[m, block, half] = jnp.where(odd == 0, high, low).astype(BF16)
        for part, step in ((0, 1), (1, -1)):
            rows = pl.ds(part * 128, 128)
            send(
                pair_send.at[m, block, :, rows, :], pair_recv.at[m, block, :, rows, :],
                r["cs_sem"].at[m, block, part], r["cr_sem"].at[m, block, part], device(dz=step),
            )

    def wait_pair(m, block):
        if WIDTH[m] == 128:
            for part in range(2):
                rows = pl.ds(part * 128, 128)
                wait(pair_recv.at[m, block, :, rows, :], r["cr_sem"].at[m, block, part])

    def value_of(m, block, half):
        if WIDTH[m] == 128:
            return pair_keep[m, block, half] + pair_recv[m, block, half].astype(F32)
        return product(m, block, half)

    def ring_send(m, slot, value, dst, step):
        dws[m][slot] = value.astype(BF16)
        send(dws[m].at[slot], dst, r["rs_sem"].at[m, slot], r["rr_sem"].at[m, slot], device(dx=step))

    def send_across(m):
        wait_pair(m, across)
        for half, step in ((0, 1), (1, -1)):
            ring_send(m, half, value_of(m, across, half), relay[m].at[half], step)

    def send_near(m):
        wait_pair(m, before)
        wait_pair(m, after)
        for half, step, block in ((0, -1, before), (1, 1, after)):
            ring_send(m, 2 + half, value_of(m, block, half), near[m].at[half], step)

    def send_far(m):
        for half, step, block in ((0, 1, after), (1, -1, before)):
            value = value_of(m, block, half)
            wait(relay[m].at[half], r["rr_sem"].at[m, half])
            ring_send(m, 4 + half, value + relay[m][half].astype(F32), far[m].at[half], step)

    def keep(m):
        wait_pair(m, x)
        for half in range(2):
            own[m][half] = value_of(m, x, half)

    def across_y(m):
        for half in range(2):
            wait(near[m].at[half], r["rr_sem"].at[m, 2 + half])
            wait(far[m].at[half], r["rr_sem"].at[m, 4 + half])

        def total(half):
            return own[m][half] + near[m][half].astype(F32) + far[m][half].astype(F32)

        ysend[m][...] = total(1 - y_hi).astype(BF16)
        send(ysend[m], yrecv[m], r["ys_sem"].at[m], r["yr_sem"].at[m], device(dy=2))
        own[m][y_hi] = total(y_hi)

    zs_sem, zr_sem = r["zs_sem"], r["zr_sem"]

    def owner_copy(m, i):
        to_z = i if WIDTH[m] == 256 else odd * 8 + i
        slot = z if WIDTH[m] == 256 else lax.div(z, 2)
        copy = pltpu.make_async_remote_copy(
            src_ref=zsend[m].at[i], dst_ref=zrecv[m].at[slot], send_sem=zs_sem.at[m, i],
            recv_sem=zr_sem.at[m, slot], device_id=device(dz=to_z - z), device_id_type=MESH,
        )
        return to_z, copy

    def from_z(m, i):
        return i if WIDTH[m] == 256 else 2 * i + lax.div(z, 8)

    def across_z(m):
        wait(yrecv[m], r["yr_sem"].at[m])
        total = own[m][y_hi] + yrecv[m][...].astype(F32)
        zsend[m][...] = total.T.astype(BF16).reshape(WIDTH[m] // 16, 16, HK)

        def post(i, carry):
            to_z, copy = owner_copy(m, i)

            @pl.when(to_z != z)
            def _():
                copy.start()

            @pl.when(to_z == z)
            def _():
                slot = z if WIDTH[m] == 256 else lax.div(z, 2)
                zrecv[m][slot] = zsend[m][i]

            return carry

        lax.fori_loop(0, WIDTH[m] // 16, post, 0)

    def owned(m):
        def arrive(i, carry):
            @pl.when(from_z(m, i) != z)
            def _():
                wait(zrecv[m].at[i], zr_sem.at[m, i])

            return carry

        lax.fori_loop(0, WIDTH[m] // 16, arrive, 0)
        total = zrecv[m][0].astype(F32)
        for i in range(1, WIDTH[m] // 16):
            total = total + zrecv[m][i].astype(F32)
        return total * (1.0 / 256.0)

    def input_grad(b, carry):
        columns = aligned(b, Q)
        block, half = lax.div(b, 2), lax.rem(b, 2)
        rows = aligned(half, Q)
        total = lax.dot_general(gn[0], w[0, block, rows, :], NT, preferred_element_type=F32)
        total += lax.dot_general(gn[1], w[1, block, rows, :], NT, preferred_element_type=F32)

        @pl.when(core == 0)
        def _():
            igk[0, :, columns] = total[0:128]
            igk[1, :, columns] = total[256:384]
            igs[0, :, columns] = total[384:512].astype(BF16)
            igs[1, :, columns] = total[128:256].astype(BF16)

        @pl.when(core == 1)
        def _():
            igk[0, :, columns] = total[384:512]
            igk[1, :, columns] = total[128:256]
            igs[0, :, columns] = total[0:128].astype(BF16)
            igs[1, :, columns] = total[256:384].astype(BF16)

        return carry

    send_across(0)
    pair(1, across)
    pair(1, before)
    pair(1, after)
    send_near(0)
    pair(1, x)
    for block in (across, before, after, x):
        pair(2, block)
    send_far(0)
    keep(0)
    send_across(1)
    send_near(1)
    lax.fori_loop(0, 4, input_grad, 0)
    send_far(1)
    across_y(0)
    send_across(2)
    send_near(2)
    keep(1)
    lax.fori_loop(4, 8, input_grad, 0)
    send(igs, igr, r["is_sem"].at[0], r["ir_sem"].at[0], device(at=other))
    across_z(0)
    send_far(2)
    keep(2)
    across_y(1)
    wait(igr, r["ir_sem"].at[0])
    for slot in (1, 0):
        igo[slot] = (igk[slot] + igr[slot].astype(F32)).astype(BF16)
    send(igo.at[1], ig_hbm.at[:, mine], r["is_sem"].at[1], r["ir_sem"].at[1], device(dy=-side))
    done = pltpu.make_async_copy(igo.at[0], ig_hbm.at[:, mine], local_sem.at[3])
    done.start()
    across_z(1)
    across_y(2)
    across_z(2)

    for m in range(3):
        final = owned(m)

        @pl.when(core == 0)
        def _():
            wg_ref[m, :, 0:HK] = final[0:8]
            fsend[m] = final[8:16]

        @pl.when(core == 1)
        def _():
            wg_ref[m, :, HK : 2 * HK] = final[8:16]
            fsend[m] = final[0:8]

    send(fsend, frecv, r["fs_sem"], r["fr_sem"], device(at=other))
    wait(frecv, r["fr_sem"])

    @pl.when(core == 0)
    def _():
        wg_ref[:, :, HK : 2 * HK] = frecv[...]

    @pl.when(core == 1)
    def _():
        wg_ref[:, :, 0:HK] = frecv[...]

    done.wait()
    wait(ig_hbm.at[:, theirs], r["ir_sem"].at[1])
    for m in range(3):

        def left(i, carry):
            to_z, copy = owner_copy(m, i)

            @pl.when(to_z != z)
            def _():
                copy.wait_send()

            return carry

        lax.fori_loop(0, WIDTH[m] // 16, left, 0)
    for src, sem in sent:
        wait(src, sem)


def local(tokens, grad_out, quant_weights, block_scales):
    any_space = pl.BlockSpec(memory_space=pl.ANY)
    vmem = pl.BlockSpec(memory_space=pltpu.VMEM)
    return pl.pallas_call(
        kernel,
        out_shape=(
            jax.ShapeDtypeStruct((TOK, 2 * HALF), BF16),
            jax.ShapeDtypeStruct((3, 8, 2 * HK), F32),
        ),
        in_specs=[any_space, any_space, any_space, vmem],
        out_specs=(any_space, vmem),
        scratch_shapes=list(scratch().values()),
        compiler_params=pltpu.CompilerParams(
            collective_id=0, has_side_effects=True, vmem_limit_bytes=56 * 1024 * 1024
        ),
    )(tokens, grad_out, quant_weights, block_scales)


def solution(mesh):
    return jax.shard_map(
        local,
        mesh=mesh,
        in_specs=(
            P(("inner", "outer"), None),
            P(("inner", "outer"), None),
            P(None, "inner", None, None),
            P(None, "inner", None),
        ),
        out_specs=(P(("inner", "outer"), None), P(None, ("inner", "outer"), None)),
        check_vma=False,
    )
```

time: 110 us -> 88.9 us (0.81)
  Pallas kernels: 106 us -> 85.1 us
    pallas_call x1, Pallas kernels: 106 us -> 85.1 us  [local(): pl.pallas_call(kernel, out_shape=(jax.ShapeDtypeStruct((TOK, 2 * HALF), B...]
where the time goes in v2:
time: 88.9 us; the launch traced here: 88.6 us
  Pallas kernels  85.1 us (96%)
  local copies, waits for them, and re-layouts  2.92 us (3%)
    pallas_call x1, Pallas kernels, local(): pl.pallas_call(kernel, out_shape=(jax.ShapeDtypeStruct((TOK, 2 * HALF), B...  85.1 us
    unnamed x4, local copies, waits for them, and re-layouts  2.92 us

profile of v2, /device:TPU:1, one launch (start us, length us, event | category | flops | bytes accessed | tf_op | source)
XLA Modules:
  0.0 88.6 jit_solution(12568420057827720357)
XLA Ops:
  0.6 85.1 %shard_map.59 = (bf16[128,4096]{1,0:T(8,128)(2,1)}, f32[3,8,512]{2,1,0:T(8,128)}) custom-call(bf16[128,4096]{1,0:T(8,128)(2,1)} %tok_hbm.1, bf16[128,4096]{1,0:T(8,128)(2,1)} %out_hbm.1, bf16[3,4,128,512]{3,2,1,0:T(8,128)(2,1)} %quant_hbm.1, f32[3,4,512]{2,1,0:T(4,128)} %scales.1), custom_call_target="tpu_custom_call" | custom-call | tf_op jit(solution)/shard_map/pallas_call | solution.py:481
  85.7 0.0 copy-start
  85.7 2.3 %copy.8 = bf16[128,4096]{1,0:T(8,128)(2,1)} copy(bf16[128,4096]{1,0:T(8,128)(2,1)} %get-tuple-element.4) | data formatting | bytes 2097152
  88.0 0.0 copy-done
  88.0 0.6 copy.9
Async XLA Ops:
  85.7 2.3 %copy-start = (f32[3,8,512]{2,1,0:T(8,128)S(1)}, f32[3,8,512]{2,1,0:T(8,128)}, u32[]{:S(2)}) copy-start(f32[3,8,512]{2,1,0:T(8,128)} %get-tuple-element.5) | copy-start | bytes 147460

commit v3 on v2

--- a/solution.py
+++ b/solution.py
@@ -21,6 +21,7 @@
     shapes = {
         "xt": vmem((4 * TOK, HALF), BF16),
         "xg": vmem((4 * TOK, HALF), BF16),
+        "away": vmem((2, TOK, HALF), BF16),
         "quant": vmem((3, 4, 128, HK), BF16),
         "w": vmem((3, NX, 512, HK), BF16),
         "pacc": vmem((3, 4 * TOK, HK), F32),
@@ -31,34 +32,34 @@
         "pair_keep": vmem((3, NX, 2, HK, 128), F32),
         "pair_send": vmem((3, NX, 2, HK, 128), BF16),
         "pair_recv": vmem((3, NX, 2, HK, 128), BF16),
-        "fsend": vmem((3, 8, HK), F32),
-        "frecv": vmem((3, 8, HK), F32),
+        "early_send": vmem((3, NX, HK, 128), BF16),
+        "early_recv": vmem((3, NX, HK, 128), BF16),
         "igk": vmem((2, TOK, HALF), F32),
         "igs": vmem((2, TOK, HALF), BF16),
         "igr": vmem((2, TOK, HALF), BF16),
         "igo": vmem((2, TOK, HALF), BF16),
-        "local_sem": dma((4,)),
+        "local_sem": dma((6,)),
         "xs_sem": dma((2, 5)), "xr_sem": dma((2, 5)),
         "ws_sem": dma((3, 10)), "wr_sem": dma((3, 10)),
         "ps_sem": dma((3, 2)), "pr_sem": dma((3, 2)),
         "cs_sem": dma((3, NX, 2)), "cr_sem": dma((3, NX, 2)),
         "rs_sem": dma((3, 6)), "rr_sem": dma((3, 6)),
-        "ys_sem": dma((3,)), "yr_sem": dma((3,)),
-        "zs_sem": dma((3, NZ)), "zr_sem": dma((3, NZ)),
+        "es_sem": dma((3, NX)), "er_sem": dma((3, NX)),
+        "ys_sem": dma, "yr_sem": dma,
+        "zs_sem": dma((3, 2)), "zr_sem": dma((3, NZ)),
         "is_sem": dma((2,)), "ir_sem": dma((2,)),
-        "fs_sem": dma, "fr_sem": dma,
     }
+    shapes |= {"ysend": vmem((HK, Q), BF16), "yrecv": vmem((HK, Q), BF16)}
     for m, width in enumerate(WIDTH):
+        piece = (width, width)
         shapes |= {
-            f"dws{m}": vmem((6, HK, width), BF16),
-            f"own{m}": vmem((2, HK, width), F32),
-            f"relay{m}": vmem((2, HK, width), BF16),
-            f"near{m}": vmem((2, HK, width), BF16),
-            f"far{m}": vmem((2, HK, width), BF16),
-            f"ysend{m}": vmem((HK, width), BF16),
-            f"yrecv{m}": vmem((HK, width), BF16),
-            f"zsend{m}": vmem((width // 16, 16, HK), BF16),
-            f"zrecv{m}": vmem((width // 16, 16, HK), BF16),
+            f"dws{m}": vmem((6, *piece), BF16),
+            f"own{m}": vmem((2, *piece), F32),
+            f"relay{m}": vmem((2, *piece), BF16),
+            f"near{m}": vmem((2, *piece), BF16),
+            f"far{m}": vmem((2, *piece), BF16),
+            f"zsend{m}": vmem((width // 16, 2, 16, 128), BF16),
+            f"zrecv{m}": vmem((width // 16, 2, 16, 128), BF16),
         }
     return shapes
 
@@ -73,17 +74,20 @@
 
 def kernel(tok_hbm, out_hbm, quant_hbm, scales, ig_hbm, wg_ref, *scratch_refs):
     r = dict(zip(scratch(), scratch_refs, strict=True))
-    xt, xg, quant, w, pacc, psend, precv, gn, gt = (
-        r[name] for name in ("xt", "xg", "quant", "w", "pacc", "psend", "precv", "gn", "gt")
+    xt, xg, away, quant, w, pacc, psend, precv, gn, gt = (
+        r[name] for name in ("xt", "xg", "away", "quant", "w", "pacc", "psend", "precv", "gn", "gt")
     )
     pair_keep, pair_send, pair_recv = r["pair_keep"], r["pair_send"], r["pair_recv"]
-    fsend, frecv, igk, igs, igr, igo = (r[name] for name in ("fsend", "frecv", "igk", "igs", "igr", "igo"))
+    igk, igs, igr, igo = (r[name] for name in ("igk", "igs", "igr", "igo"))
     local_sem, xs_sem, xr_sem, ws_sem, wr_sem = (
         r[name] for name in ("local_sem", "xs_sem", "xr_sem", "ws_sem", "wr_sem")
     )
-    dws, own, relay, near, far, ysend, yrecv, zsend, zrecv = (
+    dws, own, relay, near, far, zsend, zrecv = (
         [r[f"{name}{m}"] for m in range(3)]
-        for name in ("dws", "own", "relay", "near", "far", "ysend", "yrecv", "zsend", "zrecv")
+        for name in ("dws", "own", "relay", "near", "far", "zsend", "zrecv")
+    )
+    ysend, yrecv, early_send, early_recv = (
+        r[name] for name in ("ysend", "yrecv", "early_send", "early_recv")
     )
 
     inner, outer = lax.axis_index("inner"), lax.axis_index("outer")
@@ -108,6 +112,11 @@
 
     sent = []
 
+    def drain(count):
+        for src, sem in sent[:count]:
+            wait(src, sem)
+        del sent[:count]
+
     def send(src, dst, s_sem, r_sem, to):
         pltpu.make_async_remote_copy(
             src_ref=src, dst_ref=dst, send_sem=s_sem, recv_sem=r_sem, device_id=to, device_id_type=MESH
@@ -125,20 +134,21 @@
     pltpu.make_async_copy(quant_hbm.at[:, :, :, hidden_half], quant, local_sem.at[0]).start()
     pltpu.make_async_copy(tok_hbm.at[:, mine], xt.at[own_rows, :], local_sem.at[1]).start()
     pltpu.make_async_copy(out_hbm.at[:, mine], xg.at[own_rows, :], local_sem.at[2]).start()
+    pltpu.make_async_copy(tok_hbm.at[:, theirs], away.at[0], local_sem.at[3]).start()
+    pltpu.make_async_copy(out_hbm.at[:, theirs], away.at[1], local_sem.at[4]).start()
 
     barrier = pltpu.get_barrier_semaphore()
     partners = [
         device(at=other), device(dx=1), device(dx=-1), device(dy=1), device(dy=-1), device(dy=2),
         device(dy=side, at=other),
     ]
+    column = outer - 2 * z - core
+    for j in sorted(range(1, NZ), key=lambda j: -min(j, NZ - j)):
+        for at in range(2):
+            to = column + 2 * ((z + j) & (NZ - 1)) + at
+            pl.semaphore_signal(barrier, inc=1, device_id=(inner, to), device_id_type=MESH)
     for to in partners:
         pl.semaphore_signal(barrier, inc=1, device_id=to, device_id_type=MESH)
-
-    def greet(j, carry):
-        pl.semaphore_signal(barrier, inc=1, device_id=device(dz=j), device_id_type=MESH)
-        return carry
-
-    lax.fori_loop(1, NZ, greet, 0)
 
     def dequantise(m):
         for b in range(4):
@@ -147,17 +157,19 @@
 
     wait(quant, local_sem.at[0])
     dequantise(0)
-    pl.semaphore_wait(barrier, len(partners) + NZ - 1)
-
-    def send_tokens(a, src, dst):
+    pl.semaphore_wait(barrier, len(partners) + 2 * (NZ - 1))
+
+    def send_tokens(a, dst):
+        wait(away.at[a], local_sem.at[3 + a])
         for part in range(2):
             rows = pl.ds(part * 64, 64)
             to_rows = pl.ds(pl.multiple_of((2 - core) * TOK + part * 64, 64), 64)
             send(
-                src.at[rows, theirs], dst.at[to_rows, :], xs_sem.at[a, part], xr_sem.at[a, core],
+                away.at[a, rows, :], dst.at[to_rows, :], xs_sem.at[a, part], xr_sem.at[a, core],
                 device(dy=side, at=part),
             )
-        send(src.at[:, mine], dst.at[own_rows, :], xs_sem.at[a, 2], xr_sem.at[a, 2], device(at=other))
+        wait(dst.at[own_rows, :], local_sem.at[1 + a])
+        send(dst.at[own_rows, :], dst.at[own_rows, :], xs_sem.at[a, 2], xr_sem.at[a, 2], device(at=other))
 
     def pass_tokens(a, dst):
         for i, block in enumerate((2, 1)):
@@ -166,7 +178,6 @@
             send(dst.at[rows, :], dst.at[rows, :], xs_sem.at[a, 3 + i], xr_sem.at[a, 3 + i], device(at=other))
 
     def wait_tokens(a, dst):
-        wait(dst.at[own_rows, :], local_sem.at[1 + a])
         wait(dst.at[aligned(3 - 3 * core, TOK), :], xr_sem.at[a, 2])
         for i, block in enumerate((2, 1)):
             rows = pl.ds(pl.multiple_of(block * TOK + other * 64, 64), 64)
@@ -219,10 +230,10 @@
         send(psend.at[m, high], precv.at[m, low], r["ps_sem"].at[m, 1], r["pr_sem"].at[m, 1], device(dy=-1))
 
     send_weights(0)
-    send_tokens(0, tok_hbm, xt)
+    send_tokens(0, xt)
     dequantise(1)
     send_weights(1)
-    send_tokens(1, out_hbm, xg)
+    send_tokens(1, xg)
     dequantise(2)
     relay_weights(0)
     send_weights(2)
@@ -233,8 +244,8 @@
     relay_across(1)
     wait_tokens(0, xt)
     first_terms(0)
+    last_terms(0)
     relay_across(2)
-    last_terms(0)
     first_terms(1)
     pass_tokens(1, xg)
     last_terms(1)
@@ -278,15 +289,31 @@
                 r["cs_sem"].at[m, block, part], r["cr_sem"].at[m, block, part], device(dz=step),
             )
 
-    def wait_pair(m, block):
+    def swap_y(m, block):
+        for part in range(2):
+            rows = pl.ds(part * 128, 128)
+            wait(pair_recv.at[m, block, :, rows, :], r["cr_sem"].at[m, block, part])
+        gone = 1 - y_hi
+        early_send[m, block] = (
+            pair_keep[m, block, gone] + pair_recv[m, block, gone].astype(F32)
+        ).astype(BF16)
+        send(
+            early_send.at[m, block], early_recv.at[m, block], r["es_sem"].at[m, block], r["er_sem"].at[m, block],
+            device(dy=2),
+        )
+
+    def wait_block(m, block):
         if WIDTH[m] == 128:
-            for part in range(2):
-                rows = pl.ds(part * 128, 128)
-                wait(pair_recv.at[m, block, :, rows, :], r["cr_sem"].at[m, block, part])
+            wait(early_recv.at[m, block], r["er_sem"].at[m, block])
 
     def value_of(m, block, half):
         if WIDTH[m] == 128:
-            return pair_keep[m, block, half] + pair_recv[m, block, half].astype(F32)
+            rows = pl.ds(half * 128, 128)
+            return (
+                pair_keep[m, block, y_hi, rows, :]
+                + pair_recv[m, block, y_hi, rows, :].astype(F32)
+                + early_recv[m, block, rows, :].astype(F32)
+            )
         return product(m, block, half)
 
     def ring_send(m, slot, value, dst, step):
@@ -294,13 +321,13 @@
         send(dws[m].at[slot], dst, r["rs_sem"].at[m, slot], r["rr_sem"].at[m, slot], device(dx=step))
 
     def send_across(m):
-        wait_pair(m, across)
+        wait_block(m, across)
         for half, step in ((0, 1), (1, -1)):
             ring_send(m, half, value_of(m, across, half), relay[m].at[half], step)
 
     def send_near(m):
-        wait_pair(m, before)
-        wait_pair(m, after)
+        wait_block(m, before)
+        wait_block(m, after)
         for half, step, block in ((0, -1, before), (1, 1, after)):
             ring_send(m, 2 + half, value_of(m, block, half), near[m].at[half], step)
 
@@ -311,70 +338,108 @@
             ring_send(m, 4 + half, value + relay[m][half].astype(F32), far[m].at[half], step)
 
     def keep(m):
-        wait_pair(m, x)
+        wait_block(m, x)
         for half in range(2):
             own[m][half] = value_of(m, x, half)
 
-    def across_y(m):
+    def total_of(m, half):
+        return own[m][half] + near[m][half].astype(F32) + far[m][half].astype(F32)
+
+    def wait_ring(m):
         for half in range(2):
             wait(near[m].at[half], r["rr_sem"].at[m, 2 + half])
             wait(far[m].at[half], r["rr_sem"].at[m, 4 + half])
 
-        def total(half):
-            return own[m][half] + near[m][half].astype(F32) + far[m][half].astype(F32)
-
-        ysend[m][...] = total(1 - y_hi).astype(BF16)
-        send(ysend[m], yrecv[m], r["ys_sem"].at[m], r["yr_sem"].at[m], device(dy=2))
-        own[m][y_hi] = total(y_hi)
+    def across_y(m):
+        wait_ring(m)
+        ysend[...] = total_of(m, 1 - y_hi).astype(BF16)
+        send(ysend, yrecv, r["ys_sem"], r["yr_sem"], device(dy=2))
+        own[m][y_hi] = total_of(m, y_hi)
 
     zs_sem, zr_sem = r["zs_sem"], r["zr_sem"]
 
-    def owner_copy(m, i):
-        to_z = i if WIDTH[m] == 256 else odd * 8 + i
-        slot = z if WIDTH[m] == 256 else lax.div(z, 2)
-        copy = pltpu.make_async_remote_copy(
-            src_ref=zsend[m].at[i], dst_ref=zrecv[m].at[slot], send_sem=zs_sem.at[m, i],
-            recv_sem=zr_sem.at[m, slot], device_id=device(dz=to_z - z), device_id_type=MESH,
-        )
-        return to_z, copy
-
-    def from_z(m, i):
-        return i if WIDTH[m] == 256 else 2 * i + lax.div(z, 8)
+    def owner_of(m, i):
+        if WIDTH[m] == 256:
+            return i, z
+        return odd * 8 + i, lax.div(z, 2)
 
     def across_z(m):
-        wait(yrecv[m], r["yr_sem"].at[m])
-        total = own[m][y_hi] + yrecv[m][...].astype(F32)
-        zsend[m][...] = total.T.astype(BF16).reshape(WIDTH[m] // 16, 16, HK)
+        if WIDTH[m] == 128:
+            wait_ring(m)
+            total = jnp.concatenate([total_of(m, 0), total_of(m, 1)]).T
+        else:
+            wait(yrecv, r["yr_sem"])
+            total = (own[m][y_hi] + yrecv[...].astype(F32)).T
+        for i in range(WIDTH[m] // 16):
+            for to in range(2):
+                rows = total[16 * i + 8 * to : 16 * i + 8 * to + 8]
+                zsend[m][i, to] = jnp.concatenate([rows[:, :128], rows[:, 128:]]).astype(BF16)
 
         def post(i, carry):
-            to_z, copy = owner_copy(m, i)
+            to_z, slot = owner_of(m, i)
+
+            def copy(to, sem):
+                pltpu.make_async_remote_copy(
+                    src_ref=zsend[m].at[i, to], dst_ref=zrecv[m].at[slot, core], send_sem=zs_sem.at[m, sem],
+                    recv_sem=zr_sem.at[m, slot], device_id=device(dz=to_z - z, at=to), device_id_type=MESH,
+                ).start()
 
             @pl.when(to_z != z)
             def _():
-                copy.start()
+                copy(0, 0)
+                copy(1, 0)
 
             @pl.when(to_z == z)
             def _():
-                slot = z if WIDTH[m] == 256 else lax.div(z, 2)
-                zrecv[m][slot] = zsend[m][i]
+                copy(other, 1)
+                zrecv[m][slot, core] = zsend[m][i, core]
 
             return carry
 
         lax.fori_loop(0, WIDTH[m] // 16, post, 0)
 
     def owned(m):
+        count = WIDTH[m] // 16
+
         def arrive(i, carry):
-            @pl.when(from_z(m, i) != z)
+            from_z = i if count == NZ else 2 * i + lax.div(z, 8)
+
+            @pl.when(from_z != z)
             def _():
                 wait(zrecv[m].at[i], zr_sem.at[m, i])
 
+            @pl.when(from_z == z)
+            def _():
+                wait(zrecv[m].at[i, other], zr_sem.at[m, i])
+
             return carry
 
-        lax.fori_loop(0, WIDTH[m] // 16, arrive, 0)
-        total = zrecv[m][0].astype(F32)
-        for i in range(1, WIDTH[m] // 16):
-            total = total + zrecv[m][i].astype(F32)
-        return total * (1.0 / 256.0)
+        lax.fori_loop(0, count, arrive, 0)
+        for half in range(2):
+            total = zrecv[m][0, half].astype(F32)
+            for i in range(1, count):
+                total = total + zrecv[m][i, half].astype(F32)
+            total = total * (1.0 / 256.0)
+            for part in range(2):
+                first = half * HK + part * 128
+                wg_ref[m, :, first : first + 128] = total[8 * part : 8 * part + 8]
+
+    def left(m):
+        count = WIDTH[m] // 16
+        to_self = (odd * 8 <= z) & (z < odd * 8 + 8)
+        if count == NZ:
+            wait(zsend[m].at[pl.ds(0, NZ - 1)], zs_sem.at[m, 0])
+            wait(zsend[m].at[0, 0], zs_sem.at[m, 1])
+            return
+
+        @pl.when(to_self)
+        def _():
+            wait(zsend[m].at[pl.ds(0, count - 1)], zs_sem.at[m, 0])
+            wait(zsend[m].at[0, 0], zs_sem.at[m, 1])
+
+        @pl.when(jnp.logical_not(to_self))
+        def _():
+            wait(zsend[m], zs_sem.at[m, 0])
 
     def input_grad(b, carry):
         columns = aligned(b, Q)
@@ -399,80 +464,55 @@
 
         return carry
 
+    early = len(sent)
+    order = (across, before, after, x)
     send_across(0)
-    pair(1, across)
-    pair(1, before)
-    pair(1, after)
     send_near(0)
-    pair(1, x)
-    for block in (across, before, after, x):
-        pair(2, block)
+    for m in (1, 2):
+        for block in order:
+            pair(m, block)
+    lax.fori_loop(0, 5, input_grad, 0)
+    swap_y(1, across)
+    swap_y(1, before)
     send_far(0)
+    lax.fori_loop(5, 8, input_grad, 0)
+    send(igs, igr, r["is_sem"].at[0], r["ir_sem"].at[0], device(at=other))
+    swap_y(1, after)
+    swap_y(1, x)
     keep(0)
+    drain(early)
     send_across(1)
+    across_y(0)
+    swap_y(2, across)
+    swap_y(2, before)
     send_near(1)
-    lax.fori_loop(0, 4, input_grad, 0)
+    keep(1)
     send_far(1)
-    across_y(0)
+    swap_y(2, after)
+    swap_y(2, x)
     send_across(2)
+    across_z(1)
     send_near(2)
-    keep(1)
-    lax.fori_loop(4, 8, input_grad, 0)
-    send(igs, igr, r["is_sem"].at[0], r["ir_sem"].at[0], device(at=other))
     across_z(0)
-    send_far(2)
-    keep(2)
-    across_y(1)
     wait(igr, r["ir_sem"].at[0])
     for slot in (1, 0):
         igo[slot] = (igk[slot] + igr[slot].astype(F32)).astype(BF16)
     send(igo.at[1], ig_hbm.at[:, mine], r["is_sem"].at[1], r["ir_sem"].at[1], device(dy=-side))
-    done = pltpu.make_async_copy(igo.at[0], ig_hbm.at[:, mine], local_sem.at[3])
+    done = pltpu.make_async_copy(igo.at[0], ig_hbm.at[:, mine], local_sem.at[5])
     done.start()
-    across_z(1)
-    across_y(2)
+    drain(len(sent) - 1)
+    send_far(2)
+    keep(2)
     across_z(2)
-
-    for m in range(3):
-        final = owned(m)
-
-        @pl.when(core == 0)
-        def _():
-            wg_ref[m, :, 0:HK] = final[0:8]
-            fsend[m] = final[8:16]
-
-        @pl.when(core == 1)
-        def _():
-            wg_ref[m, :, HK : 2 * HK] = final[8:16]
-            fsend[m] = final[0:8]
-
-    send(fsend, frecv, r["fs_sem"], r["fr_sem"], device(at=other))
-    wait(frecv, r["fr_sem"])
-
-    @pl.when(core == 0)
-    def _():
-        wg_ref[:, :, HK : 2 * HK] = frecv[...]
-
-    @pl.when(core == 1)
-    def _():
-        wg_ref[:, :, 0:HK] = frecv[...]
-
+    owned(1)
+    left(1)
+    owned(0)
+    left(0)
     done.wait()
     wait(ig_hbm.at[:, theirs], r["ir_sem"].at[1])
-    for m in range(3):
-
-        def left(i, carry):
-            to_z, copy = owner_copy(m, i)
-
-            @pl.when(to_z != z)
-            def _():
-                copy.wait_send()
-
-            return carry
-
-        lax.fori_loop(0, WIDTH[m] // 16, left, 0)
-    for src, sem in sent:
-        wait(src, sem)
+    drain(len(sent))
+    left(2)
+    owned(2)
 
 
 def local(tokens, grad_out, quant_weights, block_scales):

time: 88.9 us -> 85.7 us (0.964)
  Pallas kernels: 85.1 us -> 81.9 us
    pallas_call x1, Pallas kernels: 85.1 us -> 81.9 us  [local(): pl.pallas_call(kernel, out_shape=(jax.ShapeDtypeStruct((TOK, 2 * HALF), B...]
where the time goes in v3:
time: 85.7 us; the launch traced here: 85.4 us
  Pallas kernels  81.9 us (96%)
  local copies, waits for them, and re-layouts  2.92 us (3%)
    pallas_call x1, Pallas kernels, local(): pl.pallas_call(kernel, out_shape=(jax.ShapeDtypeStruct((TOK, 2 * HALF), B...  81.9 us
    unnamed x4, local copies, waits for them, and re-layouts  2.92 us

profile of v3, /device:TPU:1, one launch (start us, length us, event | category | flops | bytes accessed | tf_op | source)
XLA Modules:
  0.0 85.4 jit_solution(8495463899084462489)
XLA Ops:
  0.6 81.9 %shard_map.59 = (bf16[128,4096]{1,0:T(8,128)(2,1)}, f32[3,8,512]{2,1,0:T(8,128)}) custom-call(bf16[128,4096]{1,0:T(8,128)(2,1)} %tok_hbm.1, bf16[128,4096]{1,0:T(8,128)(2,1)} %out_hbm.1, bf16[3,4,128,512]{3,2,1,0:T(8,128)(2,1)} %quant_hbm.1, f32[3,4,512]{2,1,0:T(4,128)} %scales.1), custom_call_target="tpu_custom_call" | custom-call | tf_op jit(solution)/shard_map/pallas_call | solution.py:521
  82.5 0.0 copy-start
  82.5 2.3 %copy.8 = bf16[128,4096]{1,0:T(8,128)(2,1)} copy(bf16[128,4096]{1,0:T(8,128)(2,1)} %get-tuple-element.4) | data formatting | bytes 2097152
  84.8 0.0 copy-done
  84.8 0.6 copy.9
Async XLA Ops:
  82.5 2.3 %copy-start = (f32[3,8,512]{2,1,0:T(8,128)S(1)}, f32[3,8,512]{2,1,0:T(8,128)}, u32[]{:S(2)}) copy-start(f32[3,8,512]{2,1,0:T(8,128)} %get-tuple-element.5) | copy-start | bytes 147460

commit v4 on v3

--- a/solution.py
+++ b/solution.py
@@ -13,6 +13,7 @@
 HK = 256
 Q = 256
 WIDTH = (256, 128, 128)
+EARLY = (False, True, True)
 NT = (((1,), (1,)), ((), ()))
 
 
@@ -45,19 +46,20 @@
         "cs_sem": dma((3, NX, 2)), "cr_sem": dma((3, NX, 2)),
         "rs_sem": dma((3, 6)), "rr_sem": dma((3, 6)),
         "es_sem": dma((3, NX)), "er_sem": dma((3, NX)),
-        "ys_sem": dma, "yr_sem": dma,
+        "ys_sem": dma((3,)), "yr_sem": dma((3,)),
         "zs_sem": dma((3, 2)), "zr_sem": dma((3, NZ)),
         "is_sem": dma((2,)), "ir_sem": dma((2,)),
     }
-    shapes |= {"ysend": vmem((HK, Q), BF16), "yrecv": vmem((HK, Q), BF16)}
     for m, width in enumerate(WIDTH):
-        piece = (width, width)
+        piece = (128 if EARLY[m] else 256, width)
         shapes |= {
             f"dws{m}": vmem((6, *piece), BF16),
             f"own{m}": vmem((2, *piece), F32),
             f"relay{m}": vmem((2, *piece), BF16),
             f"near{m}": vmem((2, *piece), BF16),
             f"far{m}": vmem((2, *piece), BF16),
+            f"ysend{m}": vmem(piece, BF16),
+            f"yrecv{m}": vmem(piece, BF16),
             f"zsend{m}": vmem((width // 16, 2, 16, 128), BF16),
             f"zrecv{m}": vmem((width // 16, 2, 16, 128), BF16),
         }
@@ -82,13 +84,11 @@
     local_sem, xs_sem, xr_sem, ws_sem, wr_sem = (
         r[name] for name in ("local_sem", "xs_sem", "xr_sem", "ws_sem", "wr_sem")
     )
-    dws, own, relay, near, far, zsend, zrecv = (
+    dws, own, relay, near, far, ysend, yrecv, zsend, zrecv = (
         [r[f"{name}{m}"] for m in range(3)]
-        for name in ("dws", "own", "relay", "near", "far", "zsend", "zrecv")
+        for name in ("dws", "own", "relay", "near", "far", "ysend", "yrecv", "zsend", "zrecv")
     )
-    ysend, yrecv, early_send, early_recv = (
-        r[name] for name in ("ysend", "yrecv", "early_send", "early_recv")
-    )
+    early_send, early_recv = r["early_send"], r["early_recv"]
 
     inner, outer = lax.axis_index("inner"), lax.axis_index("outer")
     x, y_lo = lax.rem(inner, NX), lax.div(inner, NX)
@@ -245,33 +245,37 @@
     wait_tokens(0, xt)
     first_terms(0)
     last_terms(0)
+    first_terms(1)
     relay_across(2)
-    first_terms(1)
+    last_terms(1)
     pass_tokens(1, xg)
-    last_terms(1)
     wait_tokens(1, xg)
     first_terms(2)
     last_terms(2)
 
-    for m in range(3):
+    def wait_partial(m):
         wait(precv.at[m, pl.ds(256, 256)], r["pr_sem"].at[m, 0])
         wait(precv.at[m, pl.ds(0, 256)], r["pr_sem"].at[m, 1])
 
-    def elementwise(b, carry):
+    def elementwise_hidden(b, carry):
         rows = aligned(b, 128)
-        gate, up, d_hidden = (pacc[m, rows, :] + precv[m, rows, :].astype(F32) for m in range(3))
+        gate, up = (pacc[m, rows, :] + precv[m, rows, :].astype(F32) for m in range(2))
         s = jax.nn.sigmoid(gate)
-        hidden = (gate * s * up).astype(BF16)
-        grad_up = (d_hidden * gate * s).astype(BF16)
-        grad_gate = (d_hidden * up * s * (1.0 + gate * (1.0 - s))).astype(BF16)
+        pacc[0, rows, :] = gate * s
+        pacc[1, rows, :] = up * s * (1.0 + gate * (1.0 - s))
+        gt[2, :, rows] = (gate * s * up).astype(BF16).T
+        return carry
+
+    def elementwise_grads(b, carry):
+        rows = aligned(b, 128)
+        d_hidden = pacc[2, rows, :] + precv[2, rows, :].astype(F32)
+        grad_up = (d_hidden * pacc[0, rows, :]).astype(BF16)
+        grad_gate = (d_hidden * pacc[1, rows, :]).astype(BF16)
         gn[0, rows, :] = grad_gate
         gn[1, rows, :] = grad_up
         gt[0, :, rows] = grad_gate.T
         gt[1, :, rows] = grad_up.T
-        gt[2, :, rows] = hidden.T
         return carry
-
-    lax.fori_loop(0, 4, elementwise, 0)
 
     def product(m, block, half):
         return dot(gt[m], (xg if m == 2 else xt)[:, aligned(block * 2 + half, Q)])
@@ -289,10 +293,13 @@
                 r["cs_sem"].at[m, block, part], r["cr_sem"].at[m, block, part], device(dz=step),
             )
 
-    def swap_y(m, block):
+    def wait_pair(m, block):
         for part in range(2):
             rows = pl.ds(part * 128, 128)
             wait(pair_recv.at[m, block, :, rows, :], r["cr_sem"].at[m, block, part])
+
+    def swap_y(m, block):
+        wait_pair(m, block)
         gone = 1 - y_hi
         early_send[m, block] = (
             pair_keep[m, block, gone] + pair_recv[m, block, gone].astype(F32)
@@ -303,17 +310,21 @@
         )
 
     def wait_block(m, block):
-        if WIDTH[m] == 128:
+        if EARLY[m]:
             wait(early_recv.at[m, block], r["er_sem"].at[m, block])
+        elif WIDTH[m] == 128:
+            wait_pair(m, block)
 
     def value_of(m, block, half):
-        if WIDTH[m] == 128:
+        if EARLY[m]:
             rows = pl.ds(half * 128, 128)
             return (
                 pair_keep[m, block, y_hi, rows, :]
                 + pair_recv[m, block, y_hi, rows, :].astype(F32)
                 + early_recv[m, block, rows, :].astype(F32)
             )
+        if WIDTH[m] == 128:
+            return pair_keep[m, block, half] + pair_recv[m, block, half].astype(F32)
         return product(m, block, half)
 
     def ring_send(m, slot, value, dst, step):
@@ -352,8 +363,8 @@
 
     def across_y(m):
         wait_ring(m)
-        ysend[...] = total_of(m, 1 - y_hi).astype(BF16)
-        send(ysend, yrecv, r["ys_sem"], r["yr_sem"], device(dy=2))
+        ysend[m][...] = total_of(m, 1 - y_hi).astype(BF16)
+        send(ysend[m], yrecv[m], r["ys_sem"].at[m], r["yr_sem"].at[m], device(dy=2))
         own[m][y_hi] = total_of(m, y_hi)
 
     zs_sem, zr_sem = r["zs_sem"], r["zr_sem"]
@@ -364,12 +375,12 @@
         return odd * 8 + i, lax.div(z, 2)
 
     def across_z(m):
-        if WIDTH[m] == 128:
+        if EARLY[m]:
             wait_ring(m)
             total = jnp.concatenate([total_of(m, 0), total_of(m, 1)]).T
         else:
-            wait(yrecv, r["yr_sem"])
-            total = (own[m][y_hi] + yrecv[...].astype(F32)).T
+            wait(yrecv[m], r["yr_sem"].at[m])
+            total = (own[m][y_hi] + yrecv[m][...].astype(F32)).T
         for i in range(WIDTH[m] // 16):
             for to in range(2):
                 rows = total[16 * i + 8 * to : 16 * i + 8 * to + 8]
@@ -464,55 +475,60 @@
 
         return carry
 
+    wait_partial(0)
+    wait_partial(1)
+    lax.fori_loop(0, 4, elementwise_hidden, 0)
     early = len(sent)
     order = (across, before, after, x)
+    for block in order:
+        pair(2, block)
+    swap_y(2, across)
+    wait_partial(2)
+    lax.fori_loop(0, 4, elementwise_grads, 0)
     send_across(0)
+    swap_y(2, before)
     send_near(0)
-    for m in (1, 2):
-        for block in order:
-            pair(m, block)
-    lax.fori_loop(0, 5, input_grad, 0)
+    for block in order:
+        pair(1, block)
+    swap_y(2, after)
+    swap_y(2, x)
+    lax.fori_loop(0, 4, input_grad, 0)
+    send_across(2)
     swap_y(1, across)
+    send_near(2)
     swap_y(1, before)
     send_far(0)
-    lax.fori_loop(5, 8, input_grad, 0)
+    keep(2)
+    keep(0)
+    swap_y(1, after)
+    send_far(2)
+    swap_y(1, x)
+    send_across(1)
+    lax.fori_loop(4, 8, input_grad, 0)
     send(igs, igr, r["is_sem"].at[0], r["ir_sem"].at[0], device(at=other))
-    swap_y(1, after)
-    swap_y(1, x)
-    keep(0)
     drain(early)
-    send_across(1)
     across_y(0)
-    swap_y(2, across)
-    swap_y(2, before)
     send_near(1)
+    across_z(2)
+    send_far(1)
     keep(1)
-    send_far(1)
-    swap_y(2, after)
-    swap_y(2, x)
-    send_across(2)
     across_z(1)
-    send_near(2)
-    across_z(0)
     wait(igr, r["ir_sem"].at[0])
     for slot in (1, 0):
         igo[slot] = (igk[slot] + igr[slot].astype(F32)).astype(BF16)
     send(igo.at[1], ig_hbm.at[:, mine], r["is_sem"].at[1], r["ir_sem"].at[1], device(dy=-side))
     done = pltpu.make_async_copy(igo.at[0], ig_hbm.at[:, mine], local_sem.at[5])
     done.start()
-    drain(len(sent) - 1)
-    send_far(2)
-    keep(2)
-    across_z(2)
+    across_z(0)
+    owned(2)
+    left(2)
     owned(1)
     left(1)
-    owned(0)
-    left(0)
     done.wait()
     wait(ig_hbm.at[:, theirs], r["ir_sem"].at[1])
     drain(len(sent))
-    left(2)
-    owned(2)
+    left(0)
+    owned(0)
 
 
 def local(tokens, grad_out, quant_weights, block_scales):

time: 85.7 us -> 80.7 us (0.942)
  Pallas kernels: 81.9 us -> 76.7 us
    pallas_call x1, Pallas kernels: 81.9 us -> 76.7 us  [local(): pl.pallas_call(kernel, out_shape=(jax.ShapeDtypeStruct((TOK, 2 * HALF), B...]
where the time goes in v4:
time: 80.7 us; the launch traced here: 80.3 us
  Pallas kernels  76.7 us (95%)
  local copies, waits for them, and re-layouts  2.92 us (4%)
    pallas_call x1, Pallas kernels, local(): pl.pallas_call(kernel, out_shape=(jax.ShapeDtypeStruct((TOK, 2 * HALF), B...  76.7 us
    unnamed x4, local copies, waits for them, and re-layouts  2.92 us

profile of v4, /device:TPU:1, one launch (start us, length us, event | category | flops | bytes accessed | tf_op | source)
XLA Modules:
  0.0 80.3 jit_solution(4522806646165376432)
XLA Ops:
  0.6 76.7 %shard_map.59 = (bf16[128,4096]{1,0:T(8,128)(2,1)}, f32[3,8,512]{2,1,0:T(8,128)}) custom-call(bf16[128,4096]{1,0:T(8,128)(2,1)} %tok_hbm.1, bf16[128,4096]{1,0:T(8,128)(2,1)} %out_hbm.1, bf16[3,4,128,512]{3,2,1,0:T(8,128)(2,1)} %quant_hbm.1, f32[3,4,512]{2,1,0:T(4,128)} %scales.1), custom_call_target="tpu_custom_call" | custom-call | tf_op jit(solution)/shard_map/pallas_call | solution.py:537
  77.4 0.0 copy-start
  77.4 2.3 %copy.8 = bf16[128,4096]{1,0:T(8,128)(2,1)} copy(bf16[128,4096]{1,0:T(8,128)(2,1)} %get-tuple-element.4) | data formatting | bytes 2097152
  79.7 0.0 copy-done
  79.7 0.6 copy.9
Async XLA Ops:
  77.4 2.3 %copy-start = (f32[3,8,512]{2,1,0:T(8,128)S(1)}, f32[3,8,512]{2,1,0:T(8,128)}, u32[]{:S(2)}) copy-start(f32[3,8,512]{2,1,0:T(8,128)} %get-tuple-element.5) | copy-start | bytes 147460

commit v5 on v4

--- a/solution.py
+++ b/solution.py
@@ -233,21 +233,21 @@
     send_tokens(0, xt)
     dequantise(1)
     send_weights(1)
-    send_tokens(1, xg)
     dequantise(2)
     relay_weights(0)
+    send_tokens(1, xg)
+    relay_weights(1)
     send_weights(2)
-    relay_weights(1)
     relay_across(0)
     pass_tokens(0, xt)
-    relay_weights(2)
     relay_across(1)
     wait_tokens(0, xt)
     first_terms(0)
+    relay_weights(2)
     last_terms(0)
     first_terms(1)
+    last_terms(1)
     relay_across(2)
-    last_terms(1)
     pass_tokens(1, xg)
     wait_tokens(1, xg)
     first_terms(2)

time: 80.7 us -> 78.4 us (0.971)
  Pallas kernels: 76.7 us -> 74.6 us
    pallas_call x1, Pallas kernels: 76.7 us -> 74.6 us  [local(): pl.pallas_call(kernel, out_shape=(jax.ShapeDtypeStruct((TOK, 2 * HALF), B...]
where the time goes in v5:
time: 78.4 us; the launch traced here: 78.2 us
  Pallas kernels  74.6 us (95%)
  local copies, waits for them, and re-layouts  2.92 us (4%)
    pallas_call x1, Pallas kernels, local(): pl.pallas_call(kernel, out_shape=(jax.ShapeDtypeStruct((TOK, 2 * HALF), B...  74.6 us
    unnamed x4, local copies, waits for them, and re-layouts  2.92 us

profile of v5, /device:TPU:1, one launch (start us, length us, event | category | flops | bytes accessed | tf_op | source)
XLA Modules:
  0.0 78.2 jit_solution(16651598637480079230)
XLA Ops:
  0.6 74.6 %shard_map.59 = (bf16[128,4096]{1,0:T(8,128)(2,1)}, f32[3,8,512]{2,1,0:T(8,128)}) custom-call(bf16[128,4096]{1,0:T(8,128)(2,1)} %tok_hbm.1, bf16[128,4096]{1,0:T(8,128)(2,1)} %out_hbm.1, bf16[3,4,128,512]{3,2,1,0:T(8,128)(2,1)} %quant_hbm.1, f32[3,4,512]{2,1,0:T(4,128)} %scales.1), custom_call_target="tpu_custom_call" | custom-call | tf_op jit(solution)/shard_map/pallas_call | solution.py:537
  75.3 0.0 copy-start
  75.3 2.3 %copy.8 = bf16[128,4096]{1,0:T(8,128)(2,1)} copy(bf16[128,4096]{1,0:T(8,128)(2,1)} %get-tuple-element.4) | data formatting | bytes 2097152
  77.6 0.0 copy-done
  77.6 0.6 copy.9
Async XLA Ops:
  75.3 2.3 %copy-start = (f32[3,8,512]{2,1,0:T(8,128)S(1)}, f32[3,8,512]{2,1,0:T(8,128)}, u32[]{:S(2)}) copy-start(f32[3,8,512]{2,1,0:T(8,128)} %get-tuple-element.5) | copy-start | bytes 147460

commit v6 on v5

--- a/solution.py
+++ b/solution.py
@@ -506,12 +506,12 @@
     send_across(1)
     lax.fori_loop(4, 8, input_grad, 0)
     send(igs, igr, r["is_sem"].at[0], r["ir_sem"].at[0], device(at=other))
-    drain(early)
     across_y(0)
     send_near(1)
     across_z(2)
     send_far(1)
     keep(1)
+    drain(early)
     across_z(1)
     wait(igr, r["ir_sem"].at[0])
     for slot in (1, 0):

time: 78.4 us -> 78.4 us (level)
  no operation moved by 1% of the time
where the time goes in v6:
time: 78.4 us; the launch traced here: 78.2 us
  Pallas kernels  74.6 us (95%)
  local copies, waits for them, and re-layouts  2.92 us (4%)
    pallas_call x1, Pallas kernels, local(): pl.pallas_call(kernel, out_shape=(jax.ShapeDtypeStruct((TOK, 2 * HALF), B...  74.6 us
    unnamed x4, local copies, waits for them, and re-layouts  2.92 us

profile of v6, /device:TPU:1, one launch (start us, length us, event | category | flops | bytes accessed | tf_op | source)
XLA Modules:
  0.0 78.2 jit_solution(5785141264977971527)
XLA Ops:
  0.6 74.6 %shard_map.59 = (bf16[128,4096]{1,0:T(8,128)(2,1)}, f32[3,8,512]{2,1,0:T(8,128)}) custom-call(bf16[128,4096]{1,0:T(8,128)(2,1)} %tok_hbm.1, bf16[128,4096]{1,0:T(8,128)(2,1)} %out_hbm.1, bf16[3,4,128,512]{3,2,1,0:T(8,128)(2,1)} %quant_hbm.1, f32[3,4,512]{2,1,0:T(4,128)} %scales.1), custom_call_target="tpu_custom_call" | custom-call | tf_op jit(solution)/shard_map/pallas_call | solution.py:537
  75.3 0.0 copy-start
  75.3 2.3 %copy.8 = bf16[128,4096]{1,0:T(8,128)(2,1)} copy(bf16[128,4096]{1,0:T(8,128)(2,1)} %get-tuple-element.4) | data formatting | bytes 2097152
  77.6 0.0 copy-done
  77.6 0.6 copy.9
Async XLA Ops:
  75.3 2.3 %copy-start = (f32[3,8,512]{2,1,0:T(8,128)S(1)}, f32[3,8,512]{2,1,0:T(8,128)}, u32[]{:S(2)}) copy-start(f32[3,8,512]{2,1,0:T(8,128)} %get-tuple-element.5) | copy-start | bytes 147460
